TPU v7x, 512 devices: a whole 4x8x8 slice. The times are simulated.
512 devices in a mesh: layer: 16 (over z, x_lo), dp: 32 (over x_hi, y, core).
Axes of the slice: x: 4 (x_hi: 2, x_lo: 2; x = x_hi * 2 + x_lo), y: 8, z: 8, core: 2. Of those that a mesh axis runs over, the one named last changes fastest.
Arguments:
- training_inputs: bfloat16 [16, 8192, 4096], P('layer', 'dp')
- training_output_gradient: bfloat16 [16, 8192, 4096], P('layer', 'dp')
- token_example_number: int32 [32, 256], P('dp'), may hold values from 0 to 31, never falling along the last dimension, each value on 1 to 16 neighbouring positions
- query_input_gradient: bfloat16 [16, 32, 2, 8, 4096], P('layer', 'dp'), may hold values from -6 to 6
- adapter_down_factor: bfloat16 [16, 16, 4096], P('layer')
- adapter_up_transposed: bfloat16 [16, 16, 4096], P('layer')
Outputs:
- scores: float32 [1024, 32], P('dp', 'layer')
Inputs may be any that keep to these rules, and one draw needn't show every extreme that they name: `token_example_number`: within each block the example numbers never fall, every example 0 to 31 holds 1 to 16 tokens, and some example holds exactly 16.
All inputs are finite; a program needn't handle non-finite values.
Results may differ from a plain program's by a relative error of at most 0.0092.
Values may be sent and summed in bfloat16 or wider, within the bound.
A program may use at most 128 MiB of HBM per device.

v0:
```python
import math

import jax
import jax.numpy as jnp
from jax import lax
from jax.sharding import PartitionSpec as P

EX_DEV = 32


def damped_factor(covariance):
    adapter_rank = covariance.shape[0]
    shift = 0.1 * jnp.trace(covariance) / adapter_rank
    return jnp.linalg.cholesky(covariance + shift * jnp.eye(adapter_rank, dtype=covariance.dtype))


def precondition(projected, lower_factor):
    solved = jax.scipy.linalg.cho_solve((lower_factor, True), projected.T)
    return solved.T.astype(jnp.bfloat16)


def project(token_rows, factor):
    last_dim = token_rows.ndim - 1
    return lax.dot_general(
        token_rows, factor, (((last_dim,), (1,)), ((), ())), preferred_element_type=jnp.float32
    )


def example_sums(member_table, projected, token_rows):
    row_count, example_count = member_table.shape
    spread = (member_table[:, :, None] * projected[:, None, :]).reshape(row_count, -1)
    summed = lax.dot_general(
        spread, token_rows, (((0,), (0,)), ((), ())), preferred_element_type=jnp.float32
    )
    return summed.reshape(example_count, -1).astype(jnp.bfloat16)


def form_queries(query_block, down_factor_matrix, up_factor_transposed, lower_grad, lower_act):
    query_count, _, query_len, model_width = query_block.shape
    adapter_rank = down_factor_matrix.shape[0]
    query_acts = query_block[:, 0]
    query_grads = query_block[:, 1]
    query_gproj = project(query_grads, up_factor_transposed).reshape(
        query_count * query_len, adapter_rank
    )
    query_aproj = project(query_acts, down_factor_matrix).reshape(
        query_count * query_len, adapter_rank
    )
    weighted_grad = precondition(query_gproj, lower_grad).reshape(
        query_count, query_len, adapter_rank
    )
    weighted_act = precondition(query_aproj, lower_act).reshape(
        query_count, query_len, adapter_rank
    )
    formed_a = jnp.einsum(
        "ktr,ktd->krd", weighted_grad, query_acts, preferred_element_type=jnp.float32
    )
    formed_b = jnp.einsum(
        "ktr,ktd->krd", weighted_act, query_grads, preferred_element_type=jnp.float32
    )
    flat_a = formed_a.reshape(query_count, adapter_rank * model_width)
    flat_b = formed_b.reshape(query_count, adapter_rank * model_width)
    return jnp.stack([flat_a, flat_b], axis=1).astype(jnp.bfloat16)


def local(
    training_inputs,
    training_output_gradient,
    token_example_number,
    query_input_gradient,
    adapter_down_factor,
    adapter_up_transposed,
):
    acts = training_inputs[0]
    grads = training_output_gradient[0]
    down_factor_matrix = adapter_down_factor[0]
    up_factor_transposed = adapter_up_transposed[0]
    own_queries = query_input_gradient[0]
    members = token_example_number[0]
    token_count, model_width = acts.shape
    adapter_rank = down_factor_matrix.shape[0]
    highest = lax.Precision.HIGHEST
    grad_proj = project(grads, up_factor_transposed)
    act_proj = project(acts, down_factor_matrix)
    grad_cov = jnp.dot(grad_proj.T, grad_proj, precision=highest)
    act_cov = jnp.dot(act_proj.T, act_proj, precision=highest)
    grad_cov, act_cov = lax.psum((grad_cov, act_cov), "dp")
    all_tokens = token_count * lax.axis_size("dp")
    lower_grad = damped_factor(grad_cov / all_tokens)
    lower_act = damped_factor(act_cov / all_tokens)
    example_ids = lax.broadcasted_iota(jnp.int32, (token_count, EX_DEV), 1)
    member_table = (members[:, None] == example_ids).astype(jnp.bfloat16)
    grad_a = example_sums(member_table, grad_proj.astype(jnp.bfloat16), acts)
    grad_b = example_sums(member_table, act_proj.astype(jnp.bfloat16), grads)
    own_formed = form_queries(
        own_queries, down_factor_matrix, up_factor_transposed, lower_grad, lower_act
    )
    formed = lax.all_gather(own_formed, "dp", axis=0, tiled=True)
    contract = (((1,), (1,)), ((), ()))
    first = lax.dot_general(grad_a, formed[:, 0], contract, preferred_element_type=jnp.float32)
    second = lax.dot_general(grad_b, formed[:, 1], contract, preferred_element_type=jnp.float32)
    partial_terms = first + second
    total = lax.psum(partial_terms, "layer")
    share_width = total.shape[1] // lax.axis_size("layer")
    share = lax.dynamic_slice_in_dim(total, lax.axis_index("layer") * share_width, share_width, 1)
    count_of_layers = lax.axis_size("layer") * adapter_down_factor.shape[0]
    return share / (8.0 * math.sqrt(2.0 * adapter_rank * model_width * count_of_layers))


def solution(mesh):
    placed = (
        P("layer", "dp", None),
        P("layer", "dp", None),
        P("dp", None),
        P("layer", "dp", None, None, None),
        P("layer", None, None),
        P("layer", None, None),
    )
    return jax.shard_map(
        local, mesh=mesh, in_specs=placed, out_specs=P("dp", "layer"), check_vma=False
    )
```

profile of v0, /device:TPU:24, one launch (start us, length us, event | category | flops | bytes accessed | tf_op | source)
XLA Modules:
  0.0 365.6 jit_solution(17391303109834443043)
XLA Ops:
  6.5 1.6 copy-done
  8.1 1.5 fusion.27
  9.7 0.1 fusion.29
  9.8 1.1 fusion.12
  10.9 1.1 fusion.9
  12.0 2.3 fusion.28
  14.4 117.6 %all-reduce = (f32[16,16]{0,1:T(8,128)S(1)}, f32[16,16]{0,1:T(8,128)S(1)}) all-reduce(f32[16,16]{0,1:T(8,128)S(1)} %fusion.30, f32[16,16]{0,1:T(8,128)S(1)} %fusion.29), channel_id=1, replica_groups=mesh['layer'=16,'dp'=32] {'dp'}, use_global_device_ids=true, to_apply=%region_4.7 | all-reduce | flops 512 | bytes 4096 | tf_op jit(solution)/shard_map/psum | solution.py:87
  131.9 0.7 select_reduce_fusion.3
  132.6 0.6 select_reduce_fusion.2
  134.7 1.5 cholesky.44
  136.2 0.6 compare_reduce_fusion.1
  136.8 0.6 fusion.16
  137.5 1.2 custom-call.8
  139.0 0.2 convolution_convert_fusion.3
  139.2 0.2 stack.7
  139.5 1.5 cholesky.55
  141.0 0.6 compare_reduce_fusion
  141.6 0.6 fusion.17
  142.3 1.2 custom-call.9
  143.8 0.2 convolution_convert_fusion.2
  144.1 0.2 stack.8
  144.3 1.3 pad_maximum_fusion
  145.7 3.2 convolution_convert_fusion
  148.9 5.6 %convert_element_type.52 = bf16[32,65536]{1,0:T(8,128)(2,1)} reshape(bf16[512,4096]{1,0:T(8,128)(2,1)} %convolution_convert_fusion) | data formatting | bytes 8388608 | tf_op jit(solution)/shard_map/convert_element_type | solution.py:35
  154.5 4.8 %convolution_convert_fusion.1 = bf16[512,4096]{1,0:T(8,128)(2,1)} fusion(bf16[256,512]{0,1:T(8,128)(2,1)S(1)} %bitcast.84, bf16[1,256,4096]{2,1,0:T(8,128)(2,1)} %param.9), kind=kOutput, calls=%fused_computation.1 | convolution fusion | flops 1075838976 | bytes 6553600 | tf_op jit(solution)/shard_map/dot_general | solution.py:32
  159.3 5.7 %convert_element_type.47 = bf16[32,65536]{1,0:T(8,128)(2,1)} reshape(bf16[512,4096]{1,0:T(8,128)(2,1)} %convolution_convert_fusion.1) | data formatting | bytes 8388608 | tf_op jit(solution)/shard_map/convert_element_type | solution.py:35
  164.9 100.6 %all-gather.2.cloned.1.call-done = bf16[32,2,65536]{2,1,0:T(2,128)(2,1)} async-done(((bf16[1,2,65536]{2,1,0:T(2,128)(2,1)}), bf16[32,2,65536]{2,1,0:T(2,128)(2,1)}) %all-gather.2.cloned.1.call-update) | async-done | bytes 8388624 | tf_op jit(solution)/shard_map/all_gather | solution.py:98
  265.5 16.5 %fusion.26 = (bf16[32,1,65536]{2,1,0:T(2,128)(2,1)S(1)}, bf16[32,1,65536]{2,1,0:T(2,128)(2,1)S(1)}) fusion(bf16[32,2,65536]{2,1,0:T(2,128)(2,1)} %all-gather.2.cloned.1.call-done), kind=kLoop, calls=%fused_computation.56 | loop fusion | bytes 16777216 | tf_op jit(solution)/shard_map/slice | solution.py:100
  282.0 7.4 %fusion = f32[32,32]{0,1:T(8,128)S(1)} fusion(bf16[32,65536]{1,0:T(8,128)(2,1)} %convert_element_type.52, bf16[32,1,65536]{2,1,0:T(2,128)(2,1)S(1)} %get-tuple-element.10), kind=kOutput, calls=%fused_computation.5 | convolution fusion | flops 134217728 | bytes 8392704 | tf_op jit(solution)/shard_map/dot_general | solution.py:101
  289.5 5.1 %fusion.8 = f32[32,32]{0,1:T(8,128)S(1)} fusion(f32[32,32]{0,1:T(8,128)S(1)} %fusion, bf16[32,65536]{1,0:T(8,128)(2,1)S(1)} %copy-done.1, bf16[32,1,65536]{2,1,0:T(2,128)(2,1)S(1)} %get-tuple-element.9), kind=kOutput, calls=%fused_computation.14 | convolution fusion | flops 134218752 | bytes 8396800 | tf_op jit(solution)/shard_map/dot_general | solution.py:100
  294.5 63.7 %psum.23 = f32[32,32]{0,1:T(8,128)S(1)} all-reduce(f32[32,32]{0,1:T(8,128)S(1)} %fusion.8), channel_id=1, replica_groups=mesh['layer'=16,'dp'=32] {'layer'}, use_global_device_ids=true, to_apply=%region_6.9 | all-reduce | flops 1024 | bytes 8192 | tf_op jit(solution)/shard_map/psum | solution.py:103
  358.2 0.6 dynamic-slice_multiply_fusion
  (23 shorter events, 1.0 us)
Async XLA Ops:
  6.5 1.6 copy-start
  6.5 132.4 %copy-start.2 = (bf16[1,1,2,8,4096]{4,3,2,1,0:T(8,128)(2,1)S(1)}, bf16[1,1,2,8,4096]{4,3,2,1,0:T(8,128)(2,1)}, u32[]{:S(2)}) copy-start(bf16[1,1,2,8,4096]{4,3,2,1,0:T(8,128)(2,1)} %param.12) | copy-start | bytes 393220
  6.5 139.1 %copy-start.3 = (s32[1,256]{1,0:T(1,128)S(1)}, s32[1,256]{1,0:T(1,128)}, u32[]{:S(2)}) copy-start(s32[1,256]{1,0:T(1,128)} %param.11) | copy-start | bytes 3076
  6.5 259.0 %all-gather.2.cloned.1.call-start = ((), (), s32[]{:S(2)}) async-start(), calls=%async_computation | async-start | bytes 8650752 | tf_op jit(solution)/shard_map/all_gather | solution.py:98
  282.0 7.5 %copy-start.1 = (bf16[32,65536]{1,0:T(8,128)(2,1)S(1)}, bf16[32,65536]{1,0:T(8,128)(2,1)}, u32[]{:S(2)}) copy-start(bf16[32,65536]{1,0:T(8,128)(2,1)} %convert_element_type.47) | copy-start | bytes 12582916
Sparse Core Ops, SparseCore 0:
  145.7 119.7 all-gather.1
where the time goes:
time: 367 us; the launch traced here: 366 us
  blocking collectives  181 us (49%)
  waiting for transfers between devices  101 us (28%)
  local copies, waits for them, and re-layouts  29.9 us (8%)
  matrix products  27.8 us (8%)
  between operations  14.9 us (4%)
  other arithmetic  11.2 us (3%)
    psum x1, blocking collectives, local(): grad_cov, act_cov = lax.psum((grad_cov, act_cov), 'dp')  118 us
    all_gather x1, waiting for transfers between devices, local(): formed = lax.all_gather(own_formed, 'dp', axis=0, tiled=True)  101 us
    psum x1, blocking collectives, local(): total = lax.psum(partial_terms, 'layer')  63.7 us
    slice x1, local copies, waits for them, and re-layouts, local(): formed[:, 0]  16.5 us
    convert_element_type x2, local copies, waits for them, and re-layouts, example_sums(): return summed.reshape(example_count, -1).astype(jnp.bfloat16)  11.3 us
    dot_general x2, matrix products, example_sums(): lax.dot_general(spread, token_rows, (((0,), (0,)), ((), ())), preferred_e...  8 us
    dot_general x1, matrix products, local(): lax.dot_general(grad_b, formed[:, 1], contract, preferred_element_type=jn...  7.44 us
  transfers between devices with their start and end apart: 1, of which 1 were waited for; matrix products, arithmetic and copies ran while one was open for 5% of the time, Pallas kernels for 0%

commit v1 on v0

v1 whole, which is shorter than its diff:
```python
import math

import jax
import jax.numpy as jnp
from jax import lax
from jax.experimental import pallas as pl
from jax.experimental.pallas import tpu as pltpu
from jax.sharding import PartitionSpec as P

MESH = pl.DeviceIdType.MESH
F32 = jnp.float32
BF16 = jnp.bfloat16
HIGHEST = lax.Precision.HIGHEST
NT = (((1,), (1,)), ((), ()))
NN = (((1,), (0,)), ((), ()))

TOK = 256
WIDTH = 4096
HALF = WIDTH // 2
RANK = 16
TOKENS = 8192
ROWS = 16

GROUPS = (
    ((0, 0, 0), (0, 0, 1), (0, 1, 0), (0, -1, 0), (0, 1, 1), (0, -1, 1), (1, 0, 0), (1, 0, 1)),
    ((0, 2, 0), (0, -2, 0), (0, 2, 1), (0, -2, 1), (1, 1, 0), (1, -1, 0)),
    ((0, 3, 0), (0, -3, 0), (0, 3, 1), (0, -3, 1), (1, 2, 0), (1, -2, 0), (1, 1, 1), (1, -1, 1)),
    ((0, 4, 0), (0, 4, 1), (1, 2, 1), (1, -2, 1), (1, 3, 0), (1, 3, 1)),
    ((1, -3, 0), (1, -3, 1), (1, 4, 0), (1, 4, 1)),
)
ORDER = tuple(piece for group in GROUPS for piece in group)
POS = {piece: i for i, piece in enumerate(ORDER)}
SLOTS = tuple((dx, d) for dx in (0, 1) for d in (0, 1, -1, 2, -2, 3, -3, 4))
SLOT = {slot: i for i, slot in enumerate(SLOTS)}

ONWARD = {
    (0, 0, 0): "+-x", (0, 0, 1): "+-x",
    (0, 1, 0): "+x", (0, 1, 1): "+", (0, -1, 0): "-x", (0, -1, 1): "-",
    (0, 2, 0): "+x", (0, 2, 1): "+", (0, -2, 0): "-x", (0, -2, 1): "-",
    (0, 3, 0): "x", (0, 3, 1): "x", (0, -3, 0): "-x", (0, -3, 1): "-x",
    (1, 0, 1): "+-", (1, 1, 1): "+", (1, -1, 1): "-",
    (1, 3, 0): "+", (1, 3, 1): "+",
}


def moved(piece, way):
    dx, d, p = piece
    if way == "x":
        return (1 - dx, d, p)
    d = d + 1 if way == "+" else d - 1
    return (dx, 4 if d == -4 else d, p)


def dot(a, b, dims, precision=None):
    return lax.dot_general(a, b, dims, precision=precision, preferred_element_type=F32)


def kernel(
    x_ref, g_ref, member_ref, query_ref, down_ref, up_ref, out_ref,
    xb, gb, xo, go, fm, fo, q, qo, mine, theirs, pm, ps, pown, psib,
    work, rall, vb, kst, onehot, so, rx,
    load_sem, piece_sem, send_sem, side_send, side_recv, msg_send, msg_recv, fin_send, fin_recv, known,
):
    layer, block = lax.axis_index("layer"), lax.axis_index("dp")
    xh, y, core = block // 16, (block // 2) % 8, block % 2
    z, xl = layer // 2, layer % 2

    def along_y(n):
        return (layer, xh * 16 + ((y + n + 8) % 8) * 2 + core)

    def along_z(n):
        return (((z + n + 8) % 8) * 2 + xl, block)

    partner = (layer, (1 - xh) * 16 + y * 2 + core)
    sibling = (layer, xh * 16 + y * 2 + (1 - core))
    beside = (z * 2 + (1 - xl), block)
    ways = {"+": along_y(1), "-": along_y(-1), "x": partner}

    def remote(src, dst, ssem, rsem, device):
        return pltpu.make_async_remote_copy(
            src_ref=src, dst_ref=dst, send_sem=ssem, recv_sem=rsem, device_id=device, device_id_type=MESH
        )

    def signal(sem, device):
        pl.semaphore_signal(sem, inc=1, device_id=device, device_id_type=MESH)

    def rows(piece):
        return pl.ds(POS[piece] * ROWS, ROWS)

    here = pl.ds(pl.multiple_of(core * HALF, HALF), HALF)
    there = pl.ds(pl.multiple_of((1 - core) * HALF, HALF), HALF)

    near = (
        along_y(1), along_y(-1), along_y(2), along_y(-2), partner, sibling,
        beside, along_z(1), along_z(-1), along_z(2), along_z(-2),
    )
    barrier = pltpu.get_barrier_semaphore()
    for device in near:
        signal(barrier, device)

    loads = [
        pltpu.make_async_copy(query_ref.at[:, here], q.at[rows((0, 0, 0))], load_sem.at[0]),
        pltpu.make_async_copy(query_ref.at[:, there], qo, load_sem.at[1]),
        pltpu.make_async_copy(up_ref.at[0, :, here], fm.at[pl.ds(0, RANK)], load_sem.at[2]),
        pltpu.make_async_copy(up_ref.at[0, :, there], fo.at[pl.ds(0, RANK)], load_sem.at[3]),
        pltpu.make_async_copy(down_ref.at[0, :, here], fm.at[pl.ds(RANK, RANK)], load_sem.at[4]),
        pltpu.make_async_copy(down_ref.at[0, :, there], fo.at[pl.ds(RANK, RANK)], load_sem.at[5]),
        pltpu.make_async_copy(g_ref.at[0, :, here], gb.at[pl.ds(0, TOK)], load_sem.at[6]),
        pltpu.make_async_copy(g_ref.at[0, :, there], go, load_sem.at[7]),
        pltpu.make_async_copy(x_ref.at[0, :, here], xb.at[pl.ds(0, TOK)], load_sem.at[8]),
        pltpu.make_async_copy(x_ref.at[0, :, there], xo, load_sem.at[9]),
    ]
    for copy in loads:
        copy.start()
    for copy in loads[:6]:
        copy.wait()
    own_q = dot(fm[...], q[pl.ds(0, ROWS), :], NT) + dot(fo[...], qo[...], NT)
    query_proj = jnp.concatenate([own_q[0:RANK, 8:16], own_q[RANK:, 0:8]], axis=1)
    loads[6].wait()
    loads[7].wait()
    gproj = dot(fm[0:RANK, :], gb[0:TOK, :], NT) + dot(fo[0:RANK, :], go[...], NT)
    loads[8].wait()
    loads[9].wait()
    aproj = dot(fm[RANK:, :], xb[0:TOK, :], NT) + dot(fo[RANK:, :], xo[...], NT)
    proj = jnp.concatenate([gproj, aproj], axis=0)
    cov = dot(proj, proj, NT, HIGHEST)
    both = jnp.concatenate(
        [cov[0:RANK, 0:RANK], cov[RANK:, RANK:], query_proj, jnp.zeros((RANK, 16), F32)], axis=1
    )
    mine[...] = jnp.concatenate([both[0:8], both[8:16]], axis=1)
    members = member_ref[...]
    pown[0:32, :] = proj.astype(BF16)
    pown[32:48, :] = jnp.broadcast_to(members.astype(F32), (16, TOK)).astype(BF16)
    so[...] = jnp.zeros(so.shape, F32)

    pl.semaphore_wait(barrier, len(near))

    def onward(piece):
        for way in ONWARD.get(piece, ""):
            remote(
                q.at[rows(piece)], q.at[rows(moved(piece, way))], send_sem, piece_sem.at[POS[moved(piece, way)]], ways[way]
            ).start()

    def landed(*pieces):
        for piece in pieces:
            remote(
                q.at[rows(piece)], q.at[rows(piece)], send_sem, piece_sem.at[POS[piece]], partner
            ).wait_recv()
            onward(piece)

    to_partner = remote(mine, theirs, msg_send.at[0], msg_recv.at[0], partner)
    to_partner.start()
    onward((0, 0, 0))
    side = [
        remote(qo, q.at[rows((0, 0, 1))], side_send.at[0], piece_sem.at[POS[(0, 0, 1)]], sibling),
        remote(pown, psib, side_send.at[1], side_recv.at[1], sibling),
        remote(go, gb.at[pl.ds(TOK, TOK)], side_send.at[2], side_recv.at[2], sibling),
        remote(xo, xb.at[pl.ds(TOK, TOK)], side_send.at[3], side_recv.at[3], sibling),
    ]
    for copy in side:
        copy.start()
    for device in (along_y(2), along_y(-2), along_z(2), along_z(-2)):
        signal(known.at[0], device)
    landed((0, 0, 1))

    pl.semaphore_wait(known.at[0], 4)
    signal(known.at[1], beside)
    to_partner.wait_recv()
    lane = lax.broadcasted_iota(jnp.int32, (8, 128), 1) % 64
    from_x = theirs[...]
    own = mine[...]
    pm[0] = jnp.where(lane < 32, own + from_x, jnp.where(lane < 48, own, pltpu.roll(from_x, 16, 1)))
    pair = [remote(pm.at[0], pm.at[n], msg_send.at[1], msg_recv.at[1], along_y(n)) for n in range(1, 8)]
    for copy in pair:
        copy.start()

    landed((0, 1, 0), (0, -1, 0), (1, 0, 0), (0, 1, 1), (0, -1, 1), (1, 0, 1))

    pl.semaphore_wait(known.at[1], 1)
    signal(known.at[2], sibling)
    side[1].wait_recv()
    side[2].wait_recv()
    side[3].wait_recv()

    def products(index):
        group = GROUPS[index]
        first = POS[group[0]] * ROWS
        count = len(group) * ROWS
        block_rows = q[first:first + count, :]
        with_x = dot(block_rows, xb[...], NT)
        with_g = dot(block_rows, gb[...], NT)
        for i in range(0, count, ROWS):
            kst[first + i:first + i + 8, :] = with_x[i:i + 8]
            kst[first + i + 8:first + i + 16, :] = with_g[i + 8:i + 16]

    def scores(index):
        group = GROUPS[index]
        first = POS[group[0]] * ROWS
        count = len(group) * ROWS
        weights = dot(vb[first:first + count, :], pcat(), NN)
        terms = (weights * kst[first:first + count, :]).reshape(len(group), ROWS, 2 * TOK)
        terms = jnp.sum(terms, axis=1)
        high = terms.astype(BF16)
        low = (terms - high.astype(F32)).astype(BF16)
        sums = dot(high, onehot[...], NT) + dot(low, onehot[...], NT)
        for i, (dx, d, p) in enumerate(group):
            for k in (0, 1):
                so[SLOT[dx, d], k, p:p + 1, :] = sums[i:i + 1, k * 128:(k + 1) * 128]

    def pcat():
        return jnp.concatenate([pown[0:32, :], psib[0:32, :]], axis=1)

    def send_scores(index):
        done = {piece for group in GROUPS[:index + 1] for piece in group}
        before = {piece for group in GROUPS[:index] for piece in group}
        for slot in SLOTS:
            pieces = {slot + (0,), slot + (1,)}
            if not pieces <= done or pieces <= before:
                continue
            dx, d = slot
            target = ((1 - xh) if dx else xh) * 8 + (y - d + 8) % 8
            step = (target - layer + 16) % 16
            mate = xh * 16 + y * 2 + (1 - core)

            @pl.when(step == 0)
            def _():
                rx[0] = so[SLOT[slot], 0]

            @pl.when(step != 0)
            def _():
                remote(so.at[SLOT[slot], 0], rx.at[step * 2], fin_send, fin_recv, (target, block)).start()

            remote(so.at[SLOT[slot], 1], rx.at[step * 2 + 1], fin_send, fin_recv, (target, mate)).start()

    example = lax.broadcasted_iota(jnp.int32, (128, TOK), 0)
    onehot[0:128, 0:TOK] = (example == members).astype(F32).astype(BF16)
    onehot[0:128, TOK:] = jnp.zeros((128, TOK), BF16)
    onehot[128:, 0:TOK] = jnp.zeros((128, TOK), BF16)
    others = psib[32:48, :].astype(F32)[0:1, :]
    onehot[128:, TOK:] = (example.astype(F32) == others).astype(F32).astype(BF16)

    products(0)
    landed((0, 2, 0), (0, -2, 0), (1, 1, 0), (1, -1, 0), (0, 2, 1), (0, -2, 1), (1, 1, 1), (1, -1, 1))

    remote(pm.at[pl.ds(1, 7)], pm.at[pl.ds(1, 7)], msg_send.at[1], msg_recv.at[1], sibling).wait_recv()
    across = remote(pm, ps, msg_send.at[2], msg_recv.at[2], sibling)
    across.start()
    products(1)
    landed((0, 3, 0), (0, -3, 0))

    across.wait_recv()
    total = pm[0] + ps[0]
    for n in range(1, 8):
        total = total + (pm[n] + ps[n])
    moments = jnp.concatenate([total[:, 0:32], total[:, 64:96]], axis=0) * (1.0 / TOKENS)
    for i, (dx, d, p) in enumerate(ORDER):
        source = (ps if p else pm)[(d + 8) % 8]
        at = 32 + 16 * dx
        rall[0:8, 16 * i:16 * i + 16] = source[:, at:at + 16]
        rall[8:16, 16 * i:16 * i + 16] = source[:, at + 64:at + 80]
    diagonal = (
        lax.broadcasted_iota(jnp.int32, (RANK, RANK), 0) == lax.broadcasted_iota(jnp.int32, (RANK, RANK), 1)
    ).astype(F32)
    scales = []
    for i in (0, 1):
        part = moments[:, RANK * i:RANK * (i + 1)]
        trace = jnp.sum(jnp.sum(part * diagonal, axis=1, keepdims=True), axis=0, keepdims=True)
        scale = 1.0 / trace
        scales.append(scale)
        work[i] = jnp.concatenate([part * scale + (0.1 / RANK) * diagonal, diagonal], axis=1)

    def eliminate(begin, end):
        row = lax.broadcasted_iota(jnp.int32, (RANK, 2 * RANK), 0)
        tables = [work[0], work[1]]
        for k in range(begin, end):
            for i in (0, 1):
                table = tables[i]
                pivot = table[k:k + 1, :] / table[k:k + 1, k:k + 1]
                tables[i] = jnp.where(row == k, pivot, table - table[:, k:k + 1] * pivot)
        work[0] = tables[0]
        work[1] = tables[1]

    landed((0, 3, 1), (0, -3, 1))
    eliminate(0, 4)
    landed((1, 2, 0), (1, -2, 0))
    eliminate(4, 8)
    landed((1, 2, 1), (1, -2, 1))
    eliminate(8, 12)
    landed((1, 3, 0))
    eliminate(12, 16)
    landed((1, 3, 1))
    kind = lax.broadcasted_iota(jnp.int32, (RANK, 32 * ROWS), 1) % ROWS
    solved_grad = dot(work[0][:, RANK:], rall[...] * scales[0], NN, HIGHEST)
    solved_act = dot(work[1][:, RANK:], rall[...] * scales[1], NN, HIGHEST)
    solved = jnp.concatenate(
        [jnp.where(kind < 8, solved_grad, 0.0), jnp.where(kind < 8, 0.0, solved_act)], axis=0
    )
    vb[...] = solved.T.astype(BF16)
    pl.semaphore_wait(known.at[2], 1)
    products(2)
    for index in (0, 1, 2):
        scores(index)
        send_scores(index)
    landed((0, 4, 0), (0, 4, 1))
    products(3)
    scores(3)
    send_scores(3)
    landed((1, -3, 0), (1, -3, 1), (1, 4, 0), (1, 4, 1))
    products(4)
    scores(4)
    send_scores(4)

    tail = rx.at[pl.ds(1, 31)]
    remote(tail, tail, fin_send, fin_recv, sibling).wait()
    same, other = rx[0], rx[1]
    for i in range(1, 16):
        same = same + rx[2 * i]
        other = other + rx[2 * i + 1]
    first = same[0:1, 0:32] + other[1:2, 0:32]
    second = same[1:2, 0:32] + other[0:1, 0:32]
    scale = 1.0 / (8.0 * math.sqrt(2.0 * RANK * WIDTH * 16))
    out_ref[0:1, :] = jnp.where(core == 0, first, second) * scale
    out_ref[1:2, :] = jnp.where(core == 0, second, first) * scale

    sent = q.at[pl.ds(0, 30 * ROWS)]
    remote(sent, sent, send_sem, piece_sem.at[0], partner).wait_send()
    for copy in side:
        copy.wait_send()
    to_partner.wait_send()
    remote(pm.at[pl.ds(1, 7)], pm.at[pl.ds(1, 7)], msg_send.at[1], msg_recv.at[1], sibling).wait_send()
    across.wait_send()


def local(x, g, members, queries, down, up):
    anywhere = pl.BlockSpec(memory_space=pl.ANY)
    vmem = pl.BlockSpec(memory_space=pltpu.VMEM)
    dma = pltpu.SemaphoreType.DMA
    out = pl.pallas_call(
        kernel,
        out_shape=jax.ShapeDtypeStruct((2, 32), F32),
        in_specs=[anywhere, anywhere, vmem, anywhere, anywhere, anywhere],
        out_specs=vmem,
        scratch_shapes=[
            pltpu.VMEM((2 * TOK, HALF), BF16),
            pltpu.VMEM((2 * TOK, HALF), BF16),
            pltpu.VMEM((TOK, HALF), BF16),
            pltpu.VMEM((TOK, HALF), BF16),
            pltpu.VMEM((2 * RANK, HALF), BF16),
            pltpu.VMEM((2 * RANK, HALF), BF16),
            pltpu.VMEM((32 * ROWS, HALF), BF16),
            pltpu.VMEM((ROWS, HALF), BF16),
            pltpu.VMEM((8, 128), F32),
            pltpu.VMEM((8, 128), F32),
            pltpu.VMEM((8, 8, 128), F32),
            pltpu.VMEM((8, 8, 128), F32),
            pltpu.VMEM((48, TOK), BF16),
            pltpu.VMEM((48, TOK), BF16),
            pltpu.VMEM((2, RANK, 2 * RANK), F32),
            pltpu.VMEM((RANK, 32 * ROWS), F32),
            pltpu.VMEM((32 * ROWS, 2 * RANK), BF16),
            pltpu.VMEM((32 * ROWS, 2 * TOK), F32),
            pltpu.VMEM((256, 2 * TOK), BF16),
            pltpu.VMEM((16, 2, 8, 128), F32),
            pltpu.VMEM((32, 8, 128), F32),
            dma((10,)),
            dma((32,)),
            dma,
            dma((4,)),
            dma((4,)),
            dma((3,)),
            dma((3,)),
            dma,
            dma,
            pltpu.SemaphoreType.REGULAR((3,)),
        ],
        compiler_params=pltpu.CompilerParams(
            collective_id=0, has_side_effects=True, vmem_limit_bytes=48 * 1024 * 1024
        ),
        name="influence",
    )(x, g, members, queries.reshape(ROWS, WIDTH), down, up)
    return out.T


def solution(mesh):
    placed = (
        P("layer", "dp", None),
        P("layer", "dp", None),
        P("dp", None),
        P("layer", "dp", None, None, None),
        P("layer", None, None),
        P("layer", None, None),
    )
    return jax.shard_map(
        local, mesh=mesh, in_specs=placed, out_specs=P("dp", "layer"), check_vma=False
    )
```

time: 367 us -> 50.3 us (0.14)
  the two profiles are of different devices: /device:TPU:24 before, /device:TPU:71 now
where the time goes in v1:
time: 50.3 us; the launch traced here: 50.1 us
  Pallas kernels  43 us (85%)
  local copies, waits for them, and re-layouts  7.14 us (14%)
    pallas_call x1, Pallas kernels, local(): pl.pallas_call(kernel, out_shape=jax.ShapeDtypeStruct((2, 32), F32), in_s...  43 us
    unnamed x13, local copies, waits for them, and re-layouts  7.14 us

profile of v1, /device:TPU:71, one launch (start us, length us, event | category | flops | bytes accessed | tf_op | source)
XLA Modules:
  0.0 50.1 jit_solution(4110064180434133090)
XLA Ops:
  0.0 0.0 copy-start
  0.0 1.6 %copy-done = bf16[1,256,4096]{2,1,0:T(8,128)(2,1)S(1)} copy-done((bf16[1,256,4096]{2,1,0:T(8,128)(2,1)S(1)}, bf16[1,256,4096]{2,1,0:T(8,128)(2,1)}, u32[]{:S(2)}) %copy-start) | copy-done | bytes 2097176
  1.6 0.0 copy-start.1
  1.6 1.6 %copy-done.1 = bf16[1,256,4096]{2,1,0:T(8,128)(2,1)S(1)} copy-done((bf16[1,256,4096]{2,1,0:T(8,128)(2,1)S(1)}, bf16[1,256,4096]{2,1,0:T(8,128)(2,1)}, u32[]{:S(2)}) %copy-start.1) | copy-done | bytes 2097176
  3.2 0.0 copy-start.2
  3.2 0.9 %copy-done.2 = bf16[1,1,2,8,4096]{4,3,2,1,0:T(8,128)(2,1)S(1)} copy-done((bf16[1,1,2,8,4096]{4,3,2,1,0:T(8,128)(2,1)S(1)}, bf16[1,1,2,8,4096]{4,3,2,1,0:T(8,128)(2,1)}, u32[]{:S(2)}) %copy-start.2) | copy-done | bytes 131096
  4.1 0.0 copy-start.3
  4.1 0.9 %copy-done.3 = bf16[1,16,4096]{2,1,0:T(8,128)(2,1)S(1)} copy-done((bf16[1,16,4096]{2,1,0:T(8,128)(2,1)S(1)}, bf16[1,16,4096]{2,1,0:T(8,128)(2,1)}, u32[]{:S(2)}) %copy-start.3) | copy-done | bytes 131096
  5.0 0.0 copy-start.4
  5.0 0.9 %copy-done.4 = bf16[1,16,4096]{2,1,0:T(8,128)(2,1)S(1)} copy-done((bf16[1,16,4096]{2,1,0:T(8,128)(2,1)S(1)}, bf16[1,16,4096]{2,1,0:T(8,128)(2,1)}, u32[]{:S(2)}) %copy-start.4) | copy-done | bytes 131096
  5.9 0.0 copy-start.5
  5.9 0.7 %copy-done.5 = s32[1,256]{1,0:T(1,128)S(1)} copy-done((s32[1,256]{1,0:T(1,128)S(1)}, s32[1,256]{1,0:T(1,128)}, u32[]{:S(2)}) %copy-start.5) | copy-done | bytes 1048
  6.6 43.0 %influence.1 = f32[2,32]{1,0:T(2,128)S(1)} custom-call(bf16[1,256,4096]{2,1,0:T(8,128)(2,1)S(1)} %copy-done, bf16[1,256,4096]{2,1,0:T(8,128)(2,1)S(1)} %copy-done.1, s32[1,256]{1,0:T(1,128)S(1)} %copy-done.5, bf16[16,4096]{1,0:T(8,128)(2,1)S(1)} %bitcast.2, bf16[1,16,4096]{2,1,0:T(8,128)(2,1)S(1)} %copy-done.3, bf16[1,16,4096]{2,1,0:T(8,128)(2,1)S(1)} %copy-done.4), custom_call_target="tpu_custom_call" | custom-call | tf_op jit(solution)/shard_map/influence/pallas_call | solution.py:338
  49.5 0.6 %copy.8 = f32[32,2]{0,1:T(2,128)} copy(f32[32,2]{0,1:T(2,128)S(1)} %bitcast.3) | data formatting | bytes 512
Async XLA Ops:
  0.0 1.6 %copy-start = (bf16[1,256,4096]{2,1,0:T(8,128)(2,1)S(1)}, bf16[1,256,4096]{2,1,0:T(8,128)(2,1)}, u32[]{:S(2)}) copy-start(bf16[1,256,4096]{2,1,0:T(8,128)(2,1)} %x_ref.1) | copy-start | bytes 6291460
  1.6 1.6 %copy-start.1 = (bf16[1,256,4096]{2,1,0:T(8,128)(2,1)S(1)}, bf16[1,256,4096]{2,1,0:T(8,128)(2,1)}, u32[]{:S(2)}) copy-start(bf16[1,256,4096]{2,1,0:T(8,128)(2,1)} %g_ref.1) | copy-start | bytes 6291460
  3.2 0.9 %copy-start.2 = (bf16[1,1,2,8,4096]{4,3,2,1,0:T(8,128)(2,1)S(1)}, bf16[1,1,2,8,4096]{4,3,2,1,0:T(8,128)(2,1)}, u32[]{:S(2)}) copy-start(bf16[1,1,2,8,4096]{4,3,2,1,0:T(8,128)(2,1)} %param.9) | copy-start | bytes 393220
  4.1 0.9 %copy-start.3 = (bf16[1,16,4096]{2,1,0:T(8,128)(2,1)S(1)}, bf16[1,16,4096]{2,1,0:T(8,128)(2,1)}, u32[]{:S(2)}) copy-start(bf16[1,16,4096]{2,1,0:T(8,128)(2,1)} %down_ref.1) | copy-start | bytes 393220
  5.0 0.9 %copy-start.4 = (bf16[1,16,4096]{2,1,0:T(8,128)(2,1)S(1)}, bf16[1,16,4096]{2,1,0:T(8,128)(2,1)}, u32[]{:S(2)}) copy-start(bf16[1,16,4096]{2,1,0:T(8,128)(2,1)} %up_ref.1) | copy-start | bytes 393220
  5.9 0.7 %copy-start.5 = (s32[1,256]{1,0:T(1,128)S(1)}, s32[1,256]{1,0:T(1,128)}, u32[]{:S(2)}) copy-start(s32[1,256]{1,0:T(1,128)} %member_ref.1) | copy-start | bytes 3076

commit v2 on v1

--- a/solution.py
+++ b/solution.py
@@ -59,7 +59,7 @@
     x_ref, g_ref, member_ref, query_ref, down_ref, up_ref, out_ref,
     xb, gb, xo, go, fm, fo, q, qo, mine, theirs, pm, ps, pown, psib,
     work, rall, vb, kst, onehot, so, rx,
-    load_sem, piece_sem, send_sem, side_send, side_recv, msg_send, msg_recv, fin_send, fin_recv, known,
+    mem, load_sem, piece_sem, send_sem, side_send, side_recv, msg_send, msg_recv, fin_send, fin_recv, known,
 ):
     layer, block = lax.axis_index("layer"), lax.axis_index("dp")
     xh, y, core = block // 16, (block // 2) % 8, block % 2
@@ -109,6 +109,7 @@
         pltpu.make_async_copy(g_ref.at[0, :, there], go, load_sem.at[7]),
         pltpu.make_async_copy(x_ref.at[0, :, here], xb.at[pl.ds(0, TOK)], load_sem.at[8]),
         pltpu.make_async_copy(x_ref.at[0, :, there], xo, load_sem.at[9]),
+        pltpu.make_async_copy(member_ref, mem, load_sem.at[10]),
     ]
     for copy in loads:
         copy.start()
@@ -128,7 +129,8 @@
         [cov[0:RANK, 0:RANK], cov[RANK:, RANK:], query_proj, jnp.zeros((RANK, 16), F32)], axis=1
     )
     mine[...] = jnp.concatenate([both[0:8], both[8:16]], axis=1)
-    members = member_ref[...]
+    loads[10].wait()
+    members = mem[...]
     pown[0:32, :] = proj.astype(BF16)
     pown[32:48, :] = jnp.broadcast_to(members.astype(F32), (16, TOK)).astype(BF16)
     so[...] = jnp.zeros(so.shape, F32)
@@ -332,13 +334,13 @@
 
 
 def local(x, g, members, queries, down, up):
-    anywhere = pl.BlockSpec(memory_space=pl.ANY)
+    hbm = pl.BlockSpec(memory_space=pltpu.HBM)
     vmem = pl.BlockSpec(memory_space=pltpu.VMEM)
     dma = pltpu.SemaphoreType.DMA
     out = pl.pallas_call(
         kernel,
         out_shape=jax.ShapeDtypeStruct((2, 32), F32),
-        in_specs=[anywhere, anywhere, vmem, anywhere, anywhere, anywhere],
+        in_specs=[hbm] * 6,
         out_specs=vmem,
         scratch_shapes=[
             pltpu.VMEM((2 * TOK, HALF), BF16),
@@ -362,7 +364,8 @@
             pltpu.VMEM((256, 2 * TOK), BF16),
             pltpu.VMEM((16, 2, 8, 128), F32),
             pltpu.VMEM((32, 8, 128), F32),
-            dma((10,)),
+            pltpu.VMEM((1, TOK), jnp.int32),
+            dma((11,)),
             dma((32,)),
             dma,
             dma((4,)),
@@ -374,7 +377,7 @@
             pltpu.SemaphoreType.REGULAR((3,)),
         ],
         compiler_params=pltpu.CompilerParams(
-            collective_id=0, has_side_effects=True, vmem_limit_bytes=48 * 1024 * 1024
+            collective_id=0, has_side_effects=True, vmem_limit_bytes=64 * 1024 * 1024
         ),
         name="influence",
     )(x, g, members, queries.reshape(ROWS, WIDTH), down, up)

time: 50.3 us -> 45.6 us (0.907)
  local copies, waits for them, and re-layouts: 7.14 us -> 1.24 us
  Pallas kernels: 43 us -> 44.3 us
    unnamed x13 -> x1, local copies, waits for them, and re-layouts: 7.14 us -> 1.24 us
    pallas_call x1, Pallas kernels: 43 us -> 44.3 us  [local(): pl.pallas_call(kernel, out_shape=jax.ShapeDtypeStruct((2, 32), F32), in_s...]
where the time goes in v2:
time: 45.6 us; the launch traced here: 45.5 us
  Pallas kernels  44.3 us (97%)
  local copies, waits for them, and re-layouts  1.24 us (3%)
    pallas_call x1, Pallas kernels, local(): pl.pallas_call(kernel, out_shape=jax.ShapeDtypeStruct((2, 32), F32), in_s...  44.3 us
    unnamed x1, local copies, waits for them, and re-layouts  1.24 us

profile of v2, /device:TPU:71, one launch (start us, length us, event | category | flops | bytes accessed | tf_op | source)
XLA Modules:
  0.0 45.5 jit_solution(16434162974554576522)
XLA Ops:
  0.0 44.3 %influence.1 = f32[2,32]{1,0:T(2,128)} custom-call(bf16[1,256,4096]{2,1,0:T(8,128)(2,1)} %x_ref.1, bf16[1,256,4096]{2,1,0:T(8,128)(2,1)} %g_ref.1, s32[1,256]{1,0:T(1,128)} %member_ref.1, bf16[16,4096]{1,0:T(8,128)(2,1)} %bitcast.2, bf16[1,16,4096]{2,1,0:T(8,128)(2,1)} %down_ref.1, bf16[1,16,4096]{2,1,0:T(8,128)(2,1)} %up_ref.1), custom_call_target="tpu_custom_call" | custom-call | tf_op jit(solution)/shard_map/influence/pallas_call | solution.py:340
  44.3 1.2 %copy.8 = f32[32,2]{0,1:T(2,128)} copy(f32[32,2]{0,1:T(2,128)} %bitcast.3) | data formatting | bytes 512

commit v3 on v2

v3 whole, which is shorter than its diff:
```python
import math

import jax
import jax.numpy as jnp
from jax import lax
from jax.experimental import pallas as pl
from jax.experimental.pallas import tpu as pltpu
from jax.sharding import PartitionSpec as P

MESH = pl.DeviceIdType.MESH
F32 = jnp.float32
BF16 = jnp.bfloat16
HIGHEST = lax.Precision.HIGHEST
NT = (((1,), (1,)), ((), ()))
NN = (((1,), (0,)), ((), ()))

TOK = 256
WIDTH = 4096
HALF = WIDTH // 2
RANK = 16
TOKENS = 8192
ROWS = 16

PARTS = 4
SPAN = HALF // PARTS
SLOTS = tuple((dx, d) for dx in (0, 1) for d in (0, 1, -1, 2, -2, 3, -3, 4))
SLOT = {slot: i for i, slot in enumerate(SLOTS)}

TREES = {
    (0, 0): "+-+-+-+xx-x-+-x",
    (0, 1): "+-+-+--xxxx-+x-",
    (0, 2): "+-+-+--xxxx-+--",
    (0, 3): "+-+-+-+xxxx-+x+",
    (1, 0): "+-+-+-+xxxxx+xx",
    (1, 1): "+-+-+-+xx-x-xxx",
    (1, 2): "+-+-+--xxx+xxx+",
    (1, 3): "+-+-+-+x+x+-x-x",
}

GROUPS = (
    ((0, 0, 0), (0, 0, 1), (0, 1, 0), (0, -1, 0), (1, 0, 0), (0, 1, 1), (0, -1, 1), (1, 0, 1),
     (0, 2, 0), (0, -2, 0), (1, 1, 0), (0, 2, 1)),
    ((1, -1, 0), (0, -2, 1), (1, 1, 1), (0, 3, 0), (1, -1, 1), (0, -3, 0), (0, 3, 1), (1, 2, 0),
     (1, -2, 0), (1, 2, 1), (0, -3, 1), (0, 4, 0), (1, -2, 1), (1, -3, 0)),
    ((0, 4, 1), (1, 3, 0), (1, 3, 1), (1, -3, 1), (1, 4, 1), (1, 4, 0)),
)
ORDER = tuple(query for group in GROUPS for query in group)
POS = {query: i for i, query in enumerate(ORDER)}

STEPS = (
    (0, 0, 0, 0), (0, 0, 0, 1), (0, 0, 0, 2), (0, 0, 0, 3), ("gproj",), (0, 0, 1, 0), (0, 0, 1, 1), (0, 0, 1, 2),
    (0, 0, 1, 3), ("aproj",), ("moments",), (0, 1, 0, 0), (0, -1, 0, 0), (0, 1, 0, 1), (0, -1, 0, 1), (1, 0, 0, 0),
    (0, 1, 0, 2), (0, -1, 0, 2), ("onehot",), (1, 0, 0, 1), (0, 1, 0, 3), (0, -1, 0, 3), (1, 0, 0, 2), (0, 1, 1, 0),
    (0, -1, 1, 0), (1, 0, 0, 3), (0, 1, 1, 1), (0, -1, 1, 1), (1, 0, 1, 0), (0, 1, 1, 2), (0, -1, 1, 2), (1, 0, 1, 1),
    (0, 1, 1, 3), (0, -1, 1, 3), (1, 0, 1, 2), (0, 2, 0, 0), (0, -2, 0, 0), ("pair",), (1, 0, 1, 3), (0, 2, 0, 1),
    (0, -2, 0, 1), (1, 1, 0, 0), (0, 2, 0, 2), (1, -1, 0, 0), (1, 1, 0, 1), (0, 2, 0, 3), (0, -2, 0, 2),
    (1, -1, 0, 1), (0, -2, 0, 3), (0, 2, 1, 0), (1, 1, 0, 2), (0, -2, 1, 0), (0, 2, 1, 1), ("sides",),
    ("products", 0, 0, "x"), (1, -1, 0, 2), (0, -2, 1, 1), (0, 2, 1, 2), (1, 1, 0, 3), ("products", 0, 0, "g"),
    (0, -2, 1, 2), (0, 2, 1, 3), (1, -1, 0, 3), (1, -1, 1, 1), ("products", 0, 1, "x"), (0, 3, 0, 0), (1, 1, 1, 0),
    (0, -2, 1, 3), (1, 1, 1, 3), (1, -1, 1, 0), ("products", 0, 1, "g"), (0, -3, 0, 0), (0, 3, 0, 1), (1, 1, 1, 1),
    (0, -3, 0, 1), (0, 3, 0, 2), (1, 1, 1, 2), (1, -2, 0, 0), (0, 3, 0, 3), (1, -1, 1, 2), (0, -3, 0, 2),
    (0, 3, 1, 0), (1, -1, 1, 3), (1, -2, 0, 1), (0, 3, 1, 1), (1, 2, 0, 0), (0, -3, 0, 3), (0, 3, 1, 2), (1, 2, 0, 1),
    (0, -3, 1, 0), ("across",), (0, 3, 1, 3), (1, 2, 0, 2), (1, -2, 0, 2), (1, 2, 0, 3), (0, 4, 0, 0), (0, -3, 1, 1),
    (1, 2, 1, 0), (1, 2, 1, 3), (0, -3, 1, 2), ("eliminate", 0), (1, -2, 1, 0), (1, -2, 0, 3), (1, 2, 1, 2),
    (1, 2, 1, 1), (1, -2, 1, 1), (0, 4, 0, 3), ("eliminate", 1), (1, -2, 1, 2), (0, -3, 1, 3), (0, 4, 1, 0),
    ("eliminate", 2), (1, -3, 0, 1), (0, 4, 0, 1), (0, 4, 1, 1), ("eliminate", 3), (1, -3, 0, 0), (1, 3, 0, 0),
    ("solve",), (1, 3, 1, 1), (0, 4, 0, 2), (1, 3, 0, 1), (1, -3, 0, 3), ("products", 1, 0, "x"), (1, -2, 1, 3),
    (0, 4, 1, 3), (1, 3, 1, 2), (1, -3, 0, 2), (1, 3, 0, 2), ("products", 1, 0, "g"), (1, -3, 1, 0), (0, 4, 1, 2),
    (1, 3, 0, 3), (1, 3, 1, 3), ("products", 1, 1, "x"), (1, 3, 1, 0), (1, 4, 0, 0), ("products", 1, 1, "g"),
    (1, -3, 1, 1), ("scores", 0), (1, -3, 1, 2), (1, 4, 0, 1), (1, 4, 1, 0), ("scores", 1), (1, 4, 1, 1),
    ("products", 2, 0, "x"), (1, -3, 1, 3), (1, 4, 1, 2), ("products", 2, 0, "g"), (1, 4, 0, 2), (1, 4, 0, 3),
    (1, 4, 1, 3), ("products", 2, 1, "x"), ("products", 2, 1, "g"), ("scores", 2),
)

def onward_table():
    table = {}
    for (p, h), links in TREES.items():
        for (dx, d), way in zip(SLOTS[1:], links):
            if way == "x":
                source = (1 - dx, d)
            elif way == "+":
                source = (dx, d - 1)
            else:
                source = (dx, -3 if d == 4 else d + 1)
            table.setdefault(source + (p, h), []).append((way, (dx, d, p, h)))
    return table


ONWARD = onward_table()


def dot(a, b, dims, precision=None):
    return lax.dot_general(a, b, dims, precision=precision, preferred_element_type=F32)


def kernel(
    x_ref, g_ref, member_ref, query_ref, down_ref, up_ref, out_ref,
    xb, gb, xo, go, fm, fo, q, qo, mine, theirs, pm, ps, pown, psib,
    work, rall, vb, kst, onehot, so, rx,
    mem, load_sem, piece_sem, send_sem, side_send, side_recv, msg_send, msg_recv, fin_send, fin_recv, known,
):
    layer, block = lax.axis_index("layer"), lax.axis_index("dp")
    xh, y, core = block // 16, (block // 2) % 8, block % 2
    z, xl = layer // 2, layer % 2

    def along_y(n):
        return (layer, xh * 16 + ((y + n + 8) % 8) * 2 + core)

    def along_z(n):
        return (((z + n + 8) % 8) * 2 + xl, block)

    partner = (layer, (1 - xh) * 16 + y * 2 + core)
    sibling = (layer, xh * 16 + y * 2 + (1 - core))
    beside = (z * 2 + (1 - xl), block)
    ways = {"+": along_y(1), "-": along_y(-1), "x": partner}

    def remote(src, dst, ssem, rsem, device):
        return pltpu.make_async_remote_copy(
            src_ref=src, dst_ref=dst, send_sem=ssem, recv_sem=rsem, device_id=device, device_id_type=MESH
        )

    def signal(sem, device):
        pl.semaphore_signal(sem, inc=1, device_id=device, device_id_type=MESH)

    def rows(piece):
        return pl.ds(POS[piece] * ROWS, ROWS)

    here = pl.ds(pl.multiple_of(core * HALF, HALF), HALF)
    there = pl.ds(pl.multiple_of((1 - core) * HALF, HALF), HALF)

    near = (
        along_y(1), along_y(-1), along_y(2), along_y(-2), partner, sibling,
        beside, along_z(1), along_z(-1), along_z(2), along_z(-2),
    )
    barrier = pltpu.get_barrier_semaphore()
    for device in near:
        signal(barrier, device)

    loads = [
        pltpu.make_async_copy(query_ref.at[:, here], q.at[rows((0, 0, 0))], load_sem.at[0]),
        pltpu.make_async_copy(query_ref.at[:, there], qo, load_sem.at[1]),
        pltpu.make_async_copy(up_ref.at[0, :, here], fm.at[pl.ds(0, RANK)], load_sem.at[2]),
        pltpu.make_async_copy(up_ref.at[0, :, there], fo.at[pl.ds(0, RANK)], load_sem.at[3]),
        pltpu.make_async_copy(down_ref.at[0, :, here], fm.at[pl.ds(RANK, RANK)], load_sem.at[4]),
        pltpu.make_async_copy(down_ref.at[0, :, there], fo.at[pl.ds(RANK, RANK)], load_sem.at[5]),
        pltpu.make_async_copy(g_ref.at[0, :, here], gb.at[pl.ds(0, TOK)], load_sem.at[6]),
        pltpu.make_async_copy(g_ref.at[0, :, there], go, load_sem.at[7]),
        pltpu.make_async_copy(x_ref.at[0, :, here], xb.at[pl.ds(0, TOK)], load_sem.at[8]),
        pltpu.make_async_copy(x_ref.at[0, :, there], xo, load_sem.at[9]),
        pltpu.make_async_copy(member_ref, mem, load_sem.at[10]),
    ]
    for copy in loads:
        copy.start()
    so[...] = jnp.zeros(so.shape, F32)
    loads[0].wait()
    loads[1].wait()

    pl.semaphore_wait(barrier, len(near))

    def part(query, h):
        return q.at[rows(query), pl.ds(h * SPAN, SPAN)]

    def onward(piece):
        for way, there_piece in ONWARD.get(piece, ()):
            query, h = there_piece[:3], there_piece[3]
            remote(
                part(piece[:3], h), part(query, h), send_sem, piece_sem.at[POS[query], h], ways[way]
            ).start()

    def landed(piece):
        query, h = piece[:3], piece[3]
        if query == (0, 0, 1):
            side[h].wait_recv()
        elif query != (0, 0, 0):
            remote(part(query, h), part(query, h), send_sem, piece_sem.at[POS[query], h], partner).wait_recv()
        onward(piece)

    side = [
        remote(
            qo.at[:, pl.ds(h * SPAN, SPAN)], part((0, 0, 1), h), side_send.at[h], piece_sem.at[POS[(0, 0, 1)], h], sibling
        )
        for h in range(PARTS)
    ]
    rest = [
        remote(go, gb.at[pl.ds(TOK, TOK)], side_send.at[PARTS], side_recv.at[0], sibling),
        remote(xo, xb.at[pl.ds(TOK, TOK)], side_send.at[PARTS + 1], side_recv.at[1], sibling),
        remote(pown, psib, side_send.at[PARTS + 2], side_recv.at[2], sibling),
    ]
    to_partner = remote(mine, theirs, msg_send.at[0], msg_recv.at[0], partner)
    pair = [remote(pm.at[0], pm.at[n], msg_send.at[1], msg_recv.at[1], along_y(n)) for n in range(1, 8)]
    pairs = remote(pm.at[pl.ds(1, 7)], pm.at[pl.ds(1, 7)], msg_send.at[1], msg_recv.at[1], sibling)
    across = remote(pm, ps, msg_send.at[2], msg_recv.at[2], sibling)

    def step_gproj():
        for copy in loads[2:8]:
            copy.wait()
        rest[0].start()
        projections["own"] = dot(fm[...], q[rows((0, 0, 0)), :], NT) + dot(fo[...], qo[...], NT)
        projections["grad"] = dot(fm[0:RANK, :], gb[0:TOK, :], NT) + dot(fo[0:RANK, :], go[...], NT)

    def step_aproj():
        loads[8].wait()
        loads[9].wait()
        rest[1].start()
        projections["act"] = dot(fm[RANK:, :], xb[0:TOK, :], NT) + dot(fo[RANK:, :], xo[...], NT)

    def step_moments():
        own_q = projections["own"]
        query_proj = jnp.concatenate([own_q[0:RANK, 8:16], own_q[RANK:, 0:8]], axis=1)
        proj = jnp.concatenate([projections["grad"], projections["act"]], axis=0)
        cov = dot(proj, proj, NT, HIGHEST)
        both = jnp.concatenate(
            [cov[0:RANK, 0:RANK], cov[RANK:, RANK:], query_proj, jnp.zeros((RANK, 16), F32)], axis=1
        )
        mine[...] = jnp.concatenate([both[0:8], both[8:16]], axis=1)
        to_partner.start()
        loads[10].wait()
        pown[0:32, :] = proj.astype(BF16)
        pown[32:48, :] = jnp.broadcast_to(mem[...].astype(F32), (16, TOK)).astype(BF16)
        rest[2].start()

    def step_pair():
        pl.semaphore_wait(known.at[0], 4)
        signal(known.at[1], beside)
        to_partner.wait_recv()
        lane = lax.broadcasted_iota(jnp.int32, (8, 128), 1) % 64
        from_x = theirs[...]
        own = mine[...]
        pm[0] = jnp.where(lane < 32, own + from_x, jnp.where(lane < 48, own, pltpu.roll(from_x, 16, 1)))
        for copy in pair:
            copy.start()

    def step_across():
        pl.semaphore_wait(known.at[1], 1)
        signal(known.at[2], sibling)
        pairs.wait_recv()
        across.start()

    def step_onehot():
        rest[2].wait_recv()
        example = lax.broadcasted_iota(jnp.int32, (128, TOK), 0)
        onehot[0:128, 0:TOK] = (example == mem[...]).astype(F32).astype(BF16)
        onehot[0:128, TOK:] = jnp.zeros((128, TOK), BF16)
        onehot[128:, 0:TOK] = jnp.zeros((128, TOK), BF16)
        others = psib[32:48, :].astype(F32)[0:1, :]
        onehot[128:, TOK:] = (example.astype(F32) == others).astype(F32).astype(BF16)

    def step_sides():
        rest[0].wait_recv()
        rest[1].wait_recv()

    def span(index):
        first = POS[GROUPS[index][0]] * ROWS
        return first, len(GROUPS[index]) * ROWS

    def step_products(index, h, operand):
        first, count = span(index)
        columns = slice(h * (HALF // 2), (h + 1) * (HALF // 2))
        rows_of, lift = (xb, 0) if operand == "x" else (gb, 8)
        found = dot(q[first:first + count, columns], rows_of[:, columns], NT)
        for i in range(lift, count, ROWS):
            if h == 0:
                kst[first + i:first + i + 8, :] = found[i:i + 8]
            else:
                kst[first + i:first + i + 8, :] += found[i:i + 8]

    def step_eliminate(quarter):
        if quarter == 0:
            across.wait_recv()
            total = pm[0] + ps[0]
            for n in range(1, 8):
                total = total + (pm[n] + ps[n])
            moments = jnp.concatenate([total[:, 0:32], total[:, 64:96]], axis=0) * (1.0 / TOKENS)
            for i, (dx, d, p) in enumerate(ORDER):
                source = (ps if p else pm)[(d + 8) % 8]
                at = 32 + 16 * dx
                rall[0:8, 16 * i:16 * i + 16] = source[:, at:at + 16]
                rall[8:16, 16 * i:16 * i + 16] = source[:, at + 64:at + 80]
            diagonal = (
                lax.broadcasted_iota(jnp.int32, (RANK, RANK), 0) == lax.broadcasted_iota(jnp.int32, (RANK, RANK), 1)
            ).astype(F32)
            for i in (0, 1):
                moment = moments[:, RANK * i:RANK * (i + 1)]
                trace = jnp.sum(jnp.sum(moment * diagonal, axis=1, keepdims=True), axis=0, keepdims=True)
                scales.append(1.0 / trace)
                work[i] = jnp.concatenate([moment * scales[i] + (0.1 / RANK) * diagonal, diagonal], axis=1)
        row = lax.broadcasted_iota(jnp.int32, (RANK, 2 * RANK), 0)
        tables = [work[0], work[1]]
        for k in range(4 * quarter, 4 * quarter + 4):
            for i in (0, 1):
                table = tables[i]
                pivot = table[k:k + 1, :] / table[k:k + 1, k:k + 1]
                tables[i] = jnp.where(row == k, pivot, table - table[:, k:k + 1] * pivot)
        work[0] = tables[0]
        work[1] = tables[1]

    def step_solve():
        kind = lax.broadcasted_iota(jnp.int32, (RANK, 32 * ROWS), 1) % ROWS
        solved_grad = dot(work[0][:, RANK:], rall[...] * scales[0], NN, HIGHEST)
        solved_act = dot(work[1][:, RANK:], rall[...] * scales[1], NN, HIGHEST)
        solved = jnp.concatenate(
            [jnp.where(kind < 8, solved_grad, 0.0), jnp.where(kind < 8, 0.0, solved_act)], axis=0
        )
        vb[...] = solved.T.astype(BF16)
        pl.semaphore_wait(known.at[2], 1)

    def step_scores(index):
        first, count = span(index)
        group = GROUPS[index]
        both_proj = jnp.concatenate([pown[0:32, :], psib[0:32, :]], axis=1)
        weights = dot(vb[first:first + count, :], both_proj, NN)
        terms = (weights * kst[first:first + count, :]).reshape(len(group), ROWS, 2 * TOK)
        terms = jnp.sum(terms, axis=1)
        high = terms.astype(BF16)
        low = (terms - high.astype(F32)).astype(BF16)
        sums = dot(high, onehot[...], NT) + dot(low, onehot[...], NT)
        for i, (dx, d, p) in enumerate(group):
            for k in (0, 1):
                so[SLOT[dx, d], k, p:p + 1, :] = sums[i:i + 1, k * 128:(k + 1) * 128]
        done = {query for members in GROUPS[:index + 1] for query in members}
        before = {query for members in GROUPS[:index] for query in members}
        mate = xh * 16 + y * 2 + (1 - core)
        for slot in SLOTS:
            queries = {slot + (0,), slot + (1,)}
            if not queries <= done or queries <= before:
                continue
            dx, d = slot
            target = ((1 - xh) if dx else xh) * 8 + (y - d + 8) % 8
            step = (target - layer + 16) % 16

            @pl.when(step == 0)
            def _():
                rx[0] = so[SLOT[slot], 0]

            @pl.when(step != 0)
            def _():
                remote(so.at[SLOT[slot], 0], rx.at[step * 2], fin_send, fin_recv, (target, block)).start()

            remote(so.at[SLOT[slot], 1], rx.at[step * 2 + 1], fin_send, fin_recv, (target, mate)).start()

    projections, scales = {}, []
    work_of = {
        "gproj": step_gproj, "aproj": step_aproj, "moments": step_moments, "pair": step_pair,
        "across": step_across, "onehot": step_onehot, "sides": step_sides, "products": step_products,
        "eliminate": step_eliminate, "solve": step_solve, "scores": step_scores,
    }
    started = False
    for item in STEPS:
        if isinstance(item[0], str):
            work_of[item[0]](*item[1:])
            continue
        landed(item)
        if not started and item[:3] == (0, 0, 0) and item[3] == PARTS - 1:
            started = True
            for copy in side:
                copy.start()
            for device in (along_y(2), along_y(-2), along_z(2), along_z(-2)):
                signal(known.at[0], device)

    tail = rx.at[pl.ds(1, 31)]
    remote(tail, tail, fin_send, fin_recv, sibling).wait()
    same, other = rx[0], rx[1]
    for i in range(1, 16):
        same = same + rx[2 * i]
        other = other + rx[2 * i + 1]
    first = same[0:1, 0:32] + other[1:2, 0:32]
    second = same[1:2, 0:32] + other[0:1, 0:32]
    scale = 1.0 / (8.0 * math.sqrt(2.0 * RANK * WIDTH * 16))
    out_ref[0:1, :] = jnp.where(core == 0, first, second) * scale
    out_ref[1:2, :] = jnp.where(core == 0, second, first) * scale

    sent = q.at[pl.ds(0, 30 * ROWS)]
    remote(sent, sent, send_sem, piece_sem.at[0, 0], partner).wait_send()
    for copy in side + rest:
        copy.wait_send()
    to_partner.wait_send()
    pairs.wait_send()
    across.wait_send()


def local(x, g, members, queries, down, up):
    hbm = pl.BlockSpec(memory_space=pltpu.HBM)
    vmem = pl.BlockSpec(memory_space=pltpu.VMEM)
    dma = pltpu.SemaphoreType.DMA
    out = pl.pallas_call(
        kernel,
        out_shape=jax.ShapeDtypeStruct((2, 32), F32),
        in_specs=[hbm] * 6,
        out_specs=vmem,
        scratch_shapes=[
            pltpu.VMEM((2 * TOK, HALF), BF16),
            pltpu.VMEM((2 * TOK, HALF), BF16),
            pltpu.VMEM((TOK, HALF), BF16),
            pltpu.VMEM((TOK, HALF), BF16),
            pltpu.VMEM((2 * RANK, HALF), BF16),
            pltpu.VMEM((2 * RANK, HALF), BF16),
            pltpu.VMEM((32 * ROWS, HALF), BF16),
            pltpu.VMEM((ROWS, HALF), BF16),
            pltpu.VMEM((8, 128), F32),
            pltpu.VMEM((8, 128), F32),
            pltpu.VMEM((8, 8, 128), F32),
            pltpu.VMEM((8, 8, 128), F32),
            pltpu.VMEM((48, TOK), BF16),
            pltpu.VMEM((48, TOK), BF16),
            pltpu.VMEM((2, RANK, 2 * RANK), F32),
            pltpu.VMEM((RANK, 32 * ROWS), F32),
            pltpu.VMEM((32 * ROWS, 2 * RANK), BF16),
            pltpu.VMEM((32 * ROWS, 2 * TOK), F32),
            pltpu.VMEM((256, 2 * TOK), BF16),
            pltpu.VMEM((16, 2, 8, 128), F32),
            pltpu.VMEM((32, 8, 128), F32),
            pltpu.VMEM((1, TOK), jnp.int32),
            dma((11,)),
            dma((32, PARTS)),
            dma,
            dma((PARTS + 3,)),
            dma((3,)),
            dma((3,)),
            dma((3,)),
            dma,
            dma,
            pltpu.SemaphoreType.REGULAR((3,)),
        ],
        compiler_params=pltpu.CompilerParams(
            collective_id=0, has_side_effects=True, vmem_limit_bytes=64 * 1024 * 1024
        ),
        name="influence",
    )(x, g, members, queries.reshape(ROWS, WIDTH), down, up)
    return out.T


def solution(mesh):
    placed = (
        P("layer", "dp", None),
        P("layer", "dp", None),
        P("dp", None),
        P("layer", "dp", None, None, None),
        P("layer", None, None),
        P("layer", None, None),
    )
    return jax.shard_map(
        local, mesh=mesh, in_specs=placed, out_specs=P("dp", "layer"), check_vma=False
    )
```

time: 45.6 us -> 40.7 us (0.89)
  the two profiles are of different devices: /device:TPU:71 before, /device:TPU:1 now
where the time goes in v3:
time: 40.7 us; the launch traced here: 40.3 us
  Pallas kernels  39.1 us (96%)
  local copies, waits for them, and re-layouts  1.24 us (3%)
    pallas_call x1, Pallas kernels, local(): pl.pallas_call(kernel, out_shape=jax.ShapeDtypeStruct((2, 32), F32), in_s...  39.1 us
    unnamed x1, local copies, waits for them, and re-layouts  1.24 us

profile of v3, /device:TPU:1, one launch (start us, length us, event | category | flops | bytes accessed | tf_op | source)
XLA Modules:
  0.0 40.3 jit_solution(761190135674345921)
XLA Ops:
  0.0 39.1 %influence.1 = f32[2,32]{1,0:T(2,128)} custom-call(bf16[1,256,4096]{2,1,0:T(8,128)(2,1)} %x_ref.1, bf16[1,256,4096]{2,1,0:T(8,128)(2,1)} %g_ref.1, s32[1,256]{1,0:T(1,128)} %member_ref.1, bf16[16,4096]{1,0:T(8,128)(2,1)} %bitcast.2, bf16[1,16,4096]{2,1,0:T(8,128)(2,1)} %down_ref.1, bf16[1,16,4096]{2,1,0:T(8,128)(2,1)} %up_ref.1), custom_call_target="tpu_custom_call" | custom-call | tf_op jit(solution)/shard_map/influence/pallas_call | solution.py:385
  39.1 1.2 %copy.8 = f32[32,2]{0,1:T(2,128)} copy(f32[32,2]{0,1:T(2,128)} %bitcast.3) | data formatting | bytes 512

commit v4 on v3

--- a/solution.py
+++ b/solution.py
@@ -21,72 +21,53 @@
 TOKENS = 8192
 ROWS = 16
 
-PARTS = 4
+PARTS = 2
 SPAN = HALF // PARTS
 SLOTS = tuple((dx, d) for dx in (0, 1) for d in (0, 1, -1, 2, -2, 3, -3, 4))
 SLOT = {slot: i for i, slot in enumerate(SLOTS)}
 
-TREES = {
-    (0, 0): "+-+-+-+xx-x-+-x",
-    (0, 1): "+-+-+--xxxx-+x-",
-    (0, 2): "+-+-+--xxxx-+--",
-    (0, 3): "+-+-+-+xxxx-+x+",
-    (1, 0): "+-+-+-+xxxxx+xx",
-    (1, 1): "+-+-+-+xx-x-xxx",
-    (1, 2): "+-+-+--xxx+xxx+",
-    (1, 3): "+-+-+-+x+x+-x-x",
-}
-
 GROUPS = (
     ((0, 0, 0), (0, 0, 1), (0, 1, 0), (0, -1, 0), (1, 0, 0), (0, 1, 1), (0, -1, 1), (1, 0, 1),
-     (0, 2, 0), (0, -2, 0), (1, 1, 0), (0, 2, 1)),
-    ((1, -1, 0), (0, -2, 1), (1, 1, 1), (0, 3, 0), (1, -1, 1), (0, -3, 0), (0, 3, 1), (1, 2, 0),
-     (1, -2, 0), (1, 2, 1), (0, -3, 1), (0, 4, 0), (1, -2, 1), (1, -3, 0)),
-    ((0, 4, 1), (1, 3, 0), (1, 3, 1), (1, -3, 1), (1, 4, 1), (1, 4, 0)),
+     (0, 2, 0), (0, -2, 0), (1, -1, 0), (0, 2, 1), (0, -2, 1), (1, 1, 0), (1, -1, 1), (0, -3, 0),
+     (1, 1, 1), (0, 3, 0), (0, -3, 1), (1, 2, 1), (1, 2, 0), (1, -2, 0), (0, 3, 1), (1, -2, 1)),
+    ((0, 4, 0), (0, 4, 1), (1, -3, 1), (1, 3, 1), (1, -3, 0), (1, 3, 0), (1, 4, 0), (1, 4, 1)),
 )
 ORDER = tuple(query for group in GROUPS for query in group)
 POS = {query: i for i, query in enumerate(ORDER)}
 
 STEPS = (
-    (0, 0, 0, 0), (0, 0, 0, 1), (0, 0, 0, 2), (0, 0, 0, 3), ("gproj",), (0, 0, 1, 0), (0, 0, 1, 1), (0, 0, 1, 2),
-    (0, 0, 1, 3), ("aproj",), ("moments",), (0, 1, 0, 0), (0, -1, 0, 0), (0, 1, 0, 1), (0, -1, 0, 1), (1, 0, 0, 0),
-    (0, 1, 0, 2), (0, -1, 0, 2), ("onehot",), (1, 0, 0, 1), (0, 1, 0, 3), (0, -1, 0, 3), (1, 0, 0, 2), (0, 1, 1, 0),
-    (0, -1, 1, 0), (1, 0, 0, 3), (0, 1, 1, 1), (0, -1, 1, 1), (1, 0, 1, 0), (0, 1, 1, 2), (0, -1, 1, 2), (1, 0, 1, 1),
-    (0, 1, 1, 3), (0, -1, 1, 3), (1, 0, 1, 2), (0, 2, 0, 0), (0, -2, 0, 0), ("pair",), (1, 0, 1, 3), (0, 2, 0, 1),
-    (0, -2, 0, 1), (1, 1, 0, 0), (0, 2, 0, 2), (1, -1, 0, 0), (1, 1, 0, 1), (0, 2, 0, 3), (0, -2, 0, 2),
-    (1, -1, 0, 1), (0, -2, 0, 3), (0, 2, 1, 0), (1, 1, 0, 2), (0, -2, 1, 0), (0, 2, 1, 1), ("sides",),
-    ("products", 0, 0, "x"), (1, -1, 0, 2), (0, -2, 1, 1), (0, 2, 1, 2), (1, 1, 0, 3), ("products", 0, 0, "g"),
-    (0, -2, 1, 2), (0, 2, 1, 3), (1, -1, 0, 3), (1, -1, 1, 1), ("products", 0, 1, "x"), (0, 3, 0, 0), (1, 1, 1, 0),
-    (0, -2, 1, 3), (1, 1, 1, 3), (1, -1, 1, 0), ("products", 0, 1, "g"), (0, -3, 0, 0), (0, 3, 0, 1), (1, 1, 1, 1),
-    (0, -3, 0, 1), (0, 3, 0, 2), (1, 1, 1, 2), (1, -2, 0, 0), (0, 3, 0, 3), (1, -1, 1, 2), (0, -3, 0, 2),
-    (0, 3, 1, 0), (1, -1, 1, 3), (1, -2, 0, 1), (0, 3, 1, 1), (1, 2, 0, 0), (0, -3, 0, 3), (0, 3, 1, 2), (1, 2, 0, 1),
-    (0, -3, 1, 0), ("across",), (0, 3, 1, 3), (1, 2, 0, 2), (1, -2, 0, 2), (1, 2, 0, 3), (0, 4, 0, 0), (0, -3, 1, 1),
-    (1, 2, 1, 0), (1, 2, 1, 3), (0, -3, 1, 2), ("eliminate", 0), (1, -2, 1, 0), (1, -2, 0, 3), (1, 2, 1, 2),
-    (1, 2, 1, 1), (1, -2, 1, 1), (0, 4, 0, 3), ("eliminate", 1), (1, -2, 1, 2), (0, -3, 1, 3), (0, 4, 1, 0),
-    ("eliminate", 2), (1, -3, 0, 1), (0, 4, 0, 1), (0, 4, 1, 1), ("eliminate", 3), (1, -3, 0, 0), (1, 3, 0, 0),
-    ("solve",), (1, 3, 1, 1), (0, 4, 0, 2), (1, 3, 0, 1), (1, -3, 0, 3), ("products", 1, 0, "x"), (1, -2, 1, 3),
-    (0, 4, 1, 3), (1, 3, 1, 2), (1, -3, 0, 2), (1, 3, 0, 2), ("products", 1, 0, "g"), (1, -3, 1, 0), (0, 4, 1, 2),
-    (1, 3, 0, 3), (1, 3, 1, 3), ("products", 1, 1, "x"), (1, 3, 1, 0), (1, 4, 0, 0), ("products", 1, 1, "g"),
-    (1, -3, 1, 1), ("scores", 0), (1, -3, 1, 2), (1, 4, 0, 1), (1, 4, 1, 0), ("scores", 1), (1, 4, 1, 1),
-    ("products", 2, 0, "x"), (1, -3, 1, 3), (1, 4, 1, 2), ("products", 2, 0, "g"), (1, 4, 0, 2), (1, 4, 0, 3),
-    (1, 4, 1, 3), ("products", 2, 1, "x"), ("products", 2, 1, "g"), ("scores", 2),
+    (0, 0, 0, 0), (0, 0, 0, 0, "+"), (0, 0, 0, 0, "-"), (0, 0, 0, 1), (0, 0, 0, 0, "x"), (0, 0, 0, 1, "+"),
+    (0, 0, 0, 1, "x"), (0, 0, 0, 1, "-"), (0, 0, 1, 0), (0, 0, 1, 1), (0, 0, 1, 1, "x"), (0, 0, 1, 0, "-"),
+    (0, 0, 1, 1, "+"), ("gproj",), (0, 0, 1, 0, "+"), (0, 0, 1, 1, "-"), ("aproj",), ("moments",), ("known",),
+    (0, 0, 1, 0, "x"), (0, 1, 0, 0), (0, -1, 0, 0), (0, -1, 0, 0, "-"), (0, -1, 0, 0, "x"), (0, 1, 0, 0, "+"),
+    (1, 0, 0, 0), (0, -1, 0, 1), (0, -1, 0, 1, "-"), (1, 0, 0, 0, "+"), (0, -1, 0, 1, "x"), (0, 1, 0, 1),
+    (0, 1, 0, 1, "x"), (0, 1, 1, 1), (0, -1, 1, 0), (0, -1, 1, 0, "-"), (0, 1, 1, 1, "+"), (0, -1, 1, 1),
+    (1, 0, 0, 1), (0, 1, 1, 0), (0, 1, 0, 1, "+"), (1, 0, 1, 1), (0, 1, 1, 0, "+"), (1, 0, 1, 1, "+"),
+    (0, -1, 1, 1, "x"), (0, -1, 1, 1, "-"), (0, -2, 0, 0), (0, -2, 0, 0, "-"), (0, 2, 0, 0), ("sides",),
+    (0, 1, 1, 0, "x"), ("pair",), (0, 2, 0, 0, "+"), (0, -1, 1, 0, "x"), (0, -2, 0, 1), (0, -2, 0, 1, "-"),
+    (0, -2, 1, 0), (0, -2, 1, 0, "-"), (0, 2, 1, 1), (0, 2, 1, 1, "x"), (1, -1, 0, 0), (1, -1, 0, 0, "-"),
+    (1, 1, 0, 0), (1, 1, 0, 0, "+"), ("onehot",), (0, -2, 1, 0, "x"), (0, 2, 0, 1), (0, -2, 1, 1), (0, -2, 1, 1, "-"),
+    (0, 2, 0, 1, "+"), (0, 2, 1, 0), (0, 2, 1, 0, "x"), (0, 2, 1, 0, "+"), (0, 2, 1, 1, "+"), (0, -3, 0, 0),
+    (0, -3, 0, 0, "-"), (1, -1, 1, 1), (0, -3, 0, 1), (0, -3, 0, 1, "x"), (1, 1, 0, 1), (1, -1, 0, 1), (1, 0, 1, 0),
+    (1, -1, 1, 1, "-"), (1, 1, 0, 1, "+"), (1, -1, 0, 1, "-"), (0, -3, 0, 1, "-"), (0, -3, 1, 0), (0, -3, 1, 0, "x"),
+    (1, -1, 1, 0), (1, 1, 1, 0), (1, 2, 1, 1), (1, 2, 1, 1, "+"), (0, 3, 0, 0), (1, -2, 0, 0), (0, 3, 0, 1),
+    (0, 3, 0, 1, "x"), (1, -2, 0, 0, "-"), (0, -3, 1, 1), (0, -3, 1, 1, "x"), (1, 2, 0, 0), (1, 2, 0, 0, "+"),
+    (1, 2, 1, 0), (0, 3, 1, 0), ("across",), (0, -3, 1, 1, "-"), (0, 4, 0, 0), (1, -2, 1, 0), (0, 4, 0, 0, "x"),
+    (0, 3, 1, 0, "+"), ("products", 0, 0, 1, "g"), ("products", 0, 0, 1, "x"), (1, 2, 1, 0, "+"), (1, -3, 0, 1),
+    (1, -3, 0, 1, "-"), ("eliminate", 0), (0, 3, 1, 1), (1, 1, 1, 1), (1, -2, 0, 1), (1, -2, 1, 1), (1, 2, 0, 1),
+    (1, -3, 1, 0), (1, -3, 1, 0, "-"), (1, 3, 1, 1), (1, 3, 1, 1, "+"), ("eliminate", 1), ("products", 0, 1, 2, "x"),
+    ("products", 0, 1, 2, "g"), ("eliminate", 2), ("eliminate", 3), (0, 4, 1, 0), (1, -3, 0, 0), (0, 4, 1, 1),
+    (1, 3, 0, 1), ("solve",), (1, 3, 0, 0), ("scores", 0), (1, 4, 1, 0), (0, 4, 0, 1), (1, 3, 1, 0), (1, 4, 0, 0),
+    ("products", 1, 0, 1, "x"), (1, 4, 0, 1), (1, 4, 1, 1), (1, -3, 1, 1), ("products", 1, 0, 1, "g"),
+    ("products", 1, 1, 2, "x"), ("products", 1, 1, 2, "g"), ("scores", 1),
 )
 
-def onward_table():
-    table = {}
-    for (p, h), links in TREES.items():
-        for (dx, d), way in zip(SLOTS[1:], links):
-            if way == "x":
-                source = (1 - dx, d)
-            elif way == "+":
-                source = (dx, d - 1)
-            else:
-                source = (dx, -3 if d == 4 else d + 1)
-            table.setdefault(source + (p, h), []).append((way, (dx, d, p, h)))
-    return table
-
-
-ONWARD = onward_table()
+def moved(query, way):
+    dx, d, p = query
+    if way == "x":
+        return (1 - dx, d, p)
+    d = d + 1 if way == "+" else d - 1
+    return (dx, 4 if d == -4 else d, p)
 
 
 def dot(a, b, dims, precision=None):
@@ -129,8 +110,7 @@
     there = pl.ds(pl.multiple_of((1 - core) * HALF, HALF), HALF)
 
     near = (
-        along_y(1), along_y(-1), along_y(2), along_y(-2), partner, sibling,
-        beside, along_z(1), along_z(-1), along_z(2), along_z(-2),
+        along_y(1), along_y(-1), partner, sibling, beside, along_z(1), along_z(-1),
     )
     barrier = pltpu.get_barrier_semaphore()
     for device in near:
@@ -160,20 +140,17 @@
     def part(query, h):
         return q.at[rows(query), pl.ds(h * SPAN, SPAN)]
 
-    def onward(piece):
-        for way, there_piece in ONWARD.get(piece, ()):
-            query, h = there_piece[:3], there_piece[3]
-            remote(
-                part(piece[:3], h), part(query, h), send_sem, piece_sem.at[POS[query], h], ways[way]
-            ).start()
-
-    def landed(piece):
-        query, h = piece[:3], piece[3]
+    def passed_on(query, h, way):
+        target = moved(query, way)
+        remote(
+            part(query, h), part(target, h), send_sem, piece_sem.at[POS[target], h], ways[way]
+        ).start()
+
+    def landed(query, h):
         if query == (0, 0, 1):
             side[h].wait_recv()
         elif query != (0, 0, 0):
             remote(part(query, h), part(query, h), send_sem, piece_sem.at[POS[query], h], partner).wait_recv()
-        onward(piece)
 
     side = [
         remote(
@@ -219,9 +196,14 @@
         pown[32:48, :] = jnp.broadcast_to(mem[...].astype(F32), (16, TOK)).astype(BF16)
         rest[2].start()
 
+    def step_known():
+        pl.semaphore_wait(known.at[0], 4)
+        for device in (along_y(2), along_y(-2), along_z(2), along_z(-2)):
+            signal(known.at[1], device)
+
     def step_pair():
-        pl.semaphore_wait(known.at[0], 4)
-        signal(known.at[1], beside)
+        pl.semaphore_wait(known.at[1], 4)
+        signal(known.at[2], beside)
         to_partner.wait_recv()
         lane = lax.broadcasted_iota(jnp.int32, (8, 128), 1) % 64
         from_x = theirs[...]
@@ -231,8 +213,8 @@
             copy.start()
 
     def step_across():
-        pl.semaphore_wait(known.at[1], 1)
-        signal(known.at[2], sibling)
+        pl.semaphore_wait(known.at[2], 1)
+        signal(known.at[3], sibling)
         pairs.wait_recv()
         across.start()
 
@@ -253,13 +235,13 @@
         first = POS[GROUPS[index][0]] * ROWS
         return first, len(GROUPS[index]) * ROWS
 
-    def step_products(index, h, operand):
+    def step_products(index, begin, end, operand):
         first, count = span(index)
-        columns = slice(h * (HALF // 2), (h + 1) * (HALF // 2))
+        columns = slice(begin * SPAN, end * SPAN)
         rows_of, lift = (xb, 0) if operand == "x" else (gb, 8)
         found = dot(q[first:first + count, columns], rows_of[:, columns], NT)
         for i in range(lift, count, ROWS):
-            if h == 0:
+            if begin == 0:
                 kst[first + i:first + i + 8, :] = found[i:i + 8]
             else:
                 kst[first + i:first + i + 8, :] += found[i:i + 8]
@@ -302,7 +284,7 @@
             [jnp.where(kind < 8, solved_grad, 0.0), jnp.where(kind < 8, 0.0, solved_act)], axis=0
         )
         vb[...] = solved.T.astype(BF16)
-        pl.semaphore_wait(known.at[2], 1)
+        pl.semaphore_wait(known.at[3], 1)
 
     def step_scores(index):
         first, count = span(index)
@@ -340,22 +322,21 @@
 
     projections, scales = {}, []
     work_of = {
-        "gproj": step_gproj, "aproj": step_aproj, "moments": step_moments, "pair": step_pair,
+        "gproj": step_gproj, "aproj": step_aproj, "moments": step_moments, "known": step_known, "pair": step_pair,
         "across": step_across, "onehot": step_onehot, "sides": step_sides, "products": step_products,
         "eliminate": step_eliminate, "solve": step_solve, "scores": step_scores,
     }
-    started = False
+    for copy in side:
+        copy.start()
+    for device in (along_y(1), along_y(-1), along_z(1), along_z(-1)):
+        signal(known.at[0], device)
     for item in STEPS:
         if isinstance(item[0], str):
             work_of[item[0]](*item[1:])
-            continue
-        landed(item)
-        if not started and item[:3] == (0, 0, 0) and item[3] == PARTS - 1:
-            started = True
-            for copy in side:
-                copy.start()
-            for device in (along_y(2), along_y(-2), along_z(2), along_z(-2)):
-                signal(known.at[0], device)
+        elif len(item) == 4:
+            landed(item[:3], item[3])
+        else:
+            passed_on(item[:3], item[3], item[4])
 
     tail = rx.at[pl.ds(1, 31)]
     remote(tail, tail, fin_send, fin_recv, sibling).wait()
@@ -419,7 +400,7 @@
             dma((3,)),
             dma,
             dma,
-            pltpu.SemaphoreType.REGULAR((3,)),
+            pltpu.SemaphoreType.REGULAR((4,)),
         ],
         compiler_params=pltpu.CompilerParams(
             collective_id=0, has_side_effects=True, vmem_limit_bytes=64 * 1024 * 1024

time: 40.7 us -> 39.7 us (0.975)
  Pallas kernels: 39.1 us -> 38.3 us
    pallas_call x1, Pallas kernels: 39.1 us -> 38.3 us  [local(): pl.pallas_call(kernel, out_shape=jax.ShapeDtypeStruct((2, 32), F32), in_s...]
where the time goes in v4:
time: 39.7 us; the launch traced here: 39.6 us
  Pallas kernels  38.3 us (96%)
  local copies, waits for them, and re-layouts  1.24 us (3%)
    pallas_call x1, Pallas kernels, local(): pl.pallas_call(kernel, out_shape=jax.ShapeDtypeStruct((2, 32), F32), in_s...  38.3 us
    unnamed x1, local copies, waits for them, and re-layouts  1.24 us

profile of v4, /device:TPU:1, one launch (start us, length us, event | category | flops | bytes accessed | tf_op | source)
XLA Modules:
  0.0 39.6 jit_solution(8759767656604452352)
XLA Ops:
  0.0 38.3 %influence.1 = f32[2,32]{1,0:T(2,128)} custom-call(bf16[1,256,4096]{2,1,0:T(8,128)(2,1)} %x_ref.1, bf16[1,256,4096]{2,1,0:T(8,128)(2,1)} %g_ref.1, s32[1,256]{1,0:T(1,128)} %member_ref.1, bf16[16,4096]{1,0:T(8,128)(2,1)} %bitcast.2, bf16[1,16,4096]{2,1,0:T(8,128)(2,1)} %down_ref.1, bf16[1,16,4096]{2,1,0:T(8,128)(2,1)} %up_ref.1), custom_call_target="tpu_custom_call" | custom-call | tf_op jit(solution)/shard_map/influence/pallas_call | solution.py:366
  38.3 1.2 %copy.8 = f32[32,2]{0,1:T(2,128)} copy(f32[32,2]{0,1:T(2,128)} %bitcast.3) | data formatting | bytes 512

commit v5 on v4

--- a/solution.py
+++ b/solution.py
@@ -295,7 +295,8 @@
         terms = jnp.sum(terms, axis=1)
         high = terms.astype(BF16)
         low = (terms - high.astype(F32)).astype(BF16)
-        sums = dot(high, onehot[...], NT) + dot(low, onehot[...], NT)
+        halves = dot(jnp.concatenate([high, low], axis=0), onehot[...], NT)
+        sums = halves[:len(group)] + halves[len(group):]
         for i, (dx, d, p) in enumerate(group):
             for k in (0, 1):
                 so[SLOT[dx, d], k, p:p + 1, :] = sums[i:i + 1, k * 128:(k + 1) * 128]

time: 39.7 us -> 39.5 us (level)
  no operation moved by 1% of the time
where the time goes in v5:
time: 39.5 us; the launch traced here: 39.4 us
  Pallas kernels  38.2 us (97%)
  local copies, waits for them, and re-layouts  1.24 us (3%)
    pallas_call x1, Pallas kernels, local(): pl.pallas_call(kernel, out_shape=jax.ShapeDtypeStruct((2, 32), F32), in_s...  38.2 us
    unnamed x1, local copies, waits for them, and re-layouts  1.24 us

profile of v5, /device:TPU:1, one launch (start us, length us, event | category | flops | bytes accessed | tf_op | source)
XLA Modules:
  0.0 39.4 jit_solution(5085381406039672772)
XLA Ops:
  0.0 38.2 %influence.1 = f32[2,32]{1,0:T(2,128)} custom-call(bf16[1,256,4096]{2,1,0:T(8,128)(2,1)} %x_ref.1, bf16[1,256,4096]{2,1,0:T(8,128)(2,1)} %g_ref.1, s32[1,256]{1,0:T(1,128)} %member_ref.1, bf16[16,4096]{1,0:T(8,128)(2,1)} %bitcast.2, bf16[1,16,4096]{2,1,0:T(8,128)(2,1)} %down_ref.1, bf16[1,16,4096]{2,1,0:T(8,128)(2,1)} %up_ref.1), custom_call_target="tpu_custom_call" | custom-call | tf_op jit(solution)/shard_map/influence/pallas_call | solution.py:367
  38.2 1.2 %copy.8 = f32[32,2]{0,1:T(2,128)} copy(f32[32,2]{0,1:T(2,128)} %bitcast.3) | data formatting | bytes 512
